TPU v7x, 32 devices: a whole 2x2x4 slice. The times are simulated.
32 devices in a mesh: grp: 4 (over y, x), blk: 8 (over z, core).
Axes of the slice: x: 2, y: 2, z: 4, core: 2. Of those that a mesh axis runs over, the one named last changes fastest.
Arguments:
- integrals: bfloat16 [4, 8, 10, 24, 128, 128], P('grp', 'blk'), may hold values from -6 to 6
- coefficients: bfloat16 [3072, 192], P('blk'), may hold values from -0.25 to 0.25
- tile_blocks: int32 [4, 8, 10, 2], P('grp', 'blk'), may hold values from 0 to 23
- block_owner: int32 [48], replicated, may hold values from 0 to 3, as said below
Outputs:
- owned: bfloat16 [96, 4, 4, 192, 192], P('grp', None, None, 'blk')
Inputs may be any that keep to these rules, and one draw needn't show every extreme that they name: `block_owner`: each owner holds at most 24 ij blocks, and some owner holds exactly 24.
All inputs are finite; a program needn't handle non-finite values.
Results may differ from a plain program's by a relative error of at most 0.0049.
Values may be sent and summed in bfloat16 or wider, within the bound.
A program may use at most 64 MiB of HBM per device.

v0:
```python
import jax
import jax.numpy as jnp
from jax import lax
from jax.sharding import PartitionSpec as P

NMO = 192
SB = 128
NSH = 24
R = 24
IJB = 48
CAP = 24
IPB = 4


def slot_table(block_owner, groups, capacity):
    count = block_owner.shape[0]
    order = jnp.arange(count, dtype=jnp.int32)
    same = block_owner[:, None] == block_owner[None, :]
    earlier = order[None, :] < order[:, None]
    rank = jnp.sum((same & earlier).astype(jnp.int32), axis=1)
    slot = block_owner * capacity + rank
    slots = jnp.arange(groups * capacity, dtype=jnp.int32)
    match = slot[None, :] == slots[:, None]
    source = jnp.sum(jnp.where(match, order[None, :], 0), axis=1)
    filled = jnp.any(match, axis=1)
    return (source, filled)


def body(integrals, coefficients, tile_blocks, block_owner):
    groups = lax.axis_size("grp")
    whole_coef = lax.all_gather(coefficients, "blk", axis=0, tiled=True)
    panels = whole_coef.reshape(NSH, SB, NMO)
    tiles = integrals[0, 0]
    blocks = tile_blocks[0, 0]
    la_coef = jnp.take(panels, blocks[:, 0], axis=0)
    si_coef = jnp.take(panels, blocks[:, 1], axis=0)
    quarter = jnp.einsum(
        "trab,tbj->tarj", tiles, si_coef, preferred_element_type=jnp.float32
    ).astype(jnp.bfloat16)
    half = jnp.einsum("tai,tarj->irj", la_coef, quarter, preferred_element_type=jnp.float32).astype(
        jnp.bfloat16
    )
    pair_blocks = half.reshape(IJB, IPB, R, NMO)
    source, filled = slot_table(block_owner, groups, CAP)
    everyone = lax.all_gather(pair_blocks[:, None], "grp", axis=1, tiled=True)
    mine = lax.axis_index("grp")
    wanted = lax.dynamic_slice_in_dim(source, mine * CAP, CAP, 0)
    present = lax.dynamic_slice_in_dim(filled, mine * CAP, CAP, 0)
    picked = jnp.take(everyone, wanted, axis=0)
    result = jnp.where(present[:, None, None, None, None], picked, jnp.zeros_like(picked))
    return result


def solution(mesh):
    in_specs = (
        P("grp", "blk", None, None, None, None),
        P("blk", None),
        P("grp", "blk", None, None),
        P(),
    )
    out_specs = P("grp", None, None, "blk", None)
    return jax.shard_map(body, mesh=mesh, in_specs=in_specs, out_specs=out_specs, check_vma=False)
```

profile of v0, /device:TPU:0, one launch (start us, length us, event | category | flops | bytes accessed | tf_op | source)
XLA Modules:
  0.0 164.0 jit_solution(3083706630085668082)
XLA Ops:
  6.5 0.0 all-gather.3.cloned.1.call-start
  6.5 0.7 all-gather.3.cloned.1.call-update
  7.3 0.0 all-gather.5.cloned.1.call-start
  7.3 0.8 compare_and_fusion.1
  8.1 26.6 %all-gather.3.cloned.1.call-done = bf16[3072,192]{0,1:T(8,128)(2,1)} async-done(((bf16[384,192]{0,1:T(8,128)(2,1)}), bf16[3072,192]{0,1:T(8,128)(2,1)}) %all-gather.3.cloned.1.call-update) | async-done | bytes 1179664 | tf_op jit(solution)/shard_map/all_gather | solution.py:31
  34.7 1.6 copy_bitcast_fusion
  36.3 0.6 gather_fusion.2
  36.9 0.6 gather_fusion.1
  37.6 8.7 %bitcast_convert_fusion = bf16[192,24,192]{2,0,1:T(8,128)(2,1)S(1)} fusion(bf16[10,128,192]{1,2,0:T(8,128)(2,1)S(1)} %gather_fusion.2, bf16[10,128,192]{1,2,0:T(8,128)(2,1)S(1)} %gather_fusion.1, pred[10]{0:T(512)(128)(4,1)S(1)} %get-tuple-element.12, pred[10]{0:T(512)(128)(4,1)S(1)} %get-tuple-element.8, bf16[1,1,10,24,128,128]{5,4,3,2,1,0:T(8,128)(2,1)} %param.6), kind=kOutput, calls=%fused_computation.8 | convolution fusion | flops 3782148096 | bytes 10616852 | tf_op jit(solution)/shard_map/tai,tarj->irj/dot_general | solution.py:40
  46.3 0.0 copy-start
  46.3 2.7 %copy.15 = bf16[192,24,192]{2,1,0:T(8,128)(2,1)} copy(bf16[192,24,192]{2,0,1:T(8,128)(2,1)S(1)} %bitcast_convert_fusion) | data formatting | bytes 3538944 | tf_op jit(solution)/shard_map/broadcast_in_dim;reshape | solution.py:45
  49.0 0.0 all-gather.5.cloned.1.call-update
  49.0 0.0 copy-done
  49.1 0.2 convert_reduce_fusion
  49.2 0.1 fusion.24
  49.3 0.1 dynamic_slice.6
  49.4 0.1 select_reduce_fusion
  49.5 0.1 compare_and_fusion.2
  49.6 95.6 %all-gather.5.cloned.1.call-done = bf16[48,4,4,24,192]{4,3,2,1,0:T(8,128)(2,1)} async-done(((bf16[48,1,4,24,192]{4,3,2,1,0:T(8,128)(2,1)}), bf16[48,4,4,24,192]{4,3,2,1,0:T(8,128)(2,1)}) %all-gather.5.cloned.1.call-update) | async-done | bytes 7077904 | tf_op jit(solution)/shard_map/all_gather | solution.py:45
  145.2 6.9 %gather_fusion = bf16[24,4,4,24,192]{4,3,2,1,0:T(8,128)(2,1)} fusion(bf16[48,4,4,24,192]{4,3,2,1,0:T(8,128)(2,1)} %all-gather.5.cloned.1.call-done, s32[1024]{0:T(1024)S(1)} %pad_clamp_fusion), kind=kCustom, calls=%fused_computation.2 | custom fusion | bytes 7077984 | tf_op jit(solution)/shard_map/jit(_take)/gather | solution.py:49
  152.0 5.1 %select_select_fusion = bf16[24,4,4,24,192]{4,3,2,1,0:T(8,128)(2,1)} fusion(bf16[24,4,4,24,192]{4,3,2,1,0:T(8,128)(2,1)} %gather_fusion, pred[24]{0:T(512)(128)(4,1)S(1)} %get-tuple-element.6, pred[24]{0:T(512)(128)(4,1)S(1)} %dynamic_slice.6), kind=kLoop, calls=%fused_computation.9 | loop fusion | flops 3538944 | bytes 7077936 | tf_op jit(solution)/shard_map/jit(_where)/select_n | solution.py:50
  (3 shorter events, 0.0 us)
Async XLA Ops:
  6.5 28.2 %all-gather.3.cloned.1.call-start = ((), (), s32[]{:S(2)}) async-start(), calls=%async_computation | async-start | bytes 1327104 | tf_op jit(solution)/shard_map/all_gather | solution.py:31
  7.3 137.9 %all-gather.5.cloned.1.call-start = ((), (), s32[]{:S(2)}) async-start(), calls=%async_computation.1 | async-start | bytes 11796480 | tf_op jit(solution)/shard_map/all_gather | solution.py:45
  46.3 2.8 %copy-start = (s32[48]{0:T(128)S(1)}, s32[48]{0:T(128)}, u32[]{:S(2)}) copy-start(s32[48]{0:T(128)} %param.9) | copy-start | bytes 580
Sparse Core Ops, SparseCore 0:
  9.0 25.6 all-gather.2
  49.2 95.9 all-gather.4
where the time goes:
time: 164 us
  waiting for transfers between devices  123 us (75%)
  between operations  13.5 us (8%)
  local copies, waits for them, and re-layouts  12.6 us (8%)
  matrix products  8.68 us (5%)
  other arithmetic  6.33 us (4%)
    all_gather x1, waiting for transfers between devices, body(): everyone = lax.all_gather(pair_blocks[:, None], 'grp', axis=1, tiled=True)  95.6 us
    all_gather x1, waiting for transfers between devices, body(): whole_coef = lax.all_gather(coefficients, 'blk', axis=0, tiled=True)  26.6 us
    dot_general x1, matrix products, body(): jnp.einsum('tai,tarj->irj', la_coef, quarter, preferred_element_type=jnp....  8.68 us
    gather x1, local copies, waits for them, and re-layouts, body(): picked = jnp.take(everyone, wanted, axis=0)  6.87 us
    select_n x1, other arithmetic, body(): jnp.where(present[:, None, None, None, None], picked, jnp.zeros_like(pick...  5.1 us
  transfers between devices with their start and end apart: 2, of which 2 were waited for; matrix products, arithmetic and copies ran while one was open for 1% of the time, Pallas kernels for 0%

commit v1 on v0

v1 whole, which is shorter than its diff:
```python
import functools
import math

import jax
import jax.numpy as jnp
from jax import lax
from jax.experimental import pallas as pl
from jax.experimental.pallas import tpu as pltpu
from jax.sharding import PartitionSpec as P

NMO = 192
SB = 128
KT = 10
R = 24
IJB = 48
CAP = 24
IPB = 4
LANE = 128
HALF = NMO - LANE
SG = 3
WIDE = CAP * IPB
PACK = WIDE + WIDE // 2
RC = 2
NCH = R // RC
MESH = pl.DeviceIdType.MESH
BF = jnp.bfloat16
F32 = jnp.float32


def exchange(
    n_grp, n_blk, ints, coef, tile_blocks, owner, out,
    iv, table, panels, si, lat, quarter, send,
    int_sem, own_sem, gs_sem, gr_sem, fs_sem, fr_sem, s_sem, r_sem, l_sem,
):
    g = lax.axis_index("grp")
    b = lax.axis_index("blk")
    z = b // 2
    c = b % 2
    sib = z * 2 + (1 - c)
    n_z = n_blk // 2
    depth, unit = coef.shape[0], coef.shape[1]

    load = pltpu.make_async_copy(ints, iv, int_sem)
    load.start()

    def rows(blk):
        return pl.ds(blk * depth, depth)

    keep = pltpu.make_async_copy(coef, table.at[rows(b)], own_sem)
    keep.start()

    barrier = pltpu.get_barrier_semaphore()
    for k in range(1, n_z):
        pl.semaphore_signal(barrier, inc=1, device_id=(g, lax.rem(z + k, n_z) * 2 + c), device_id_type=MESH)
    pl.semaphore_signal(barrier, inc=1, device_id=(g, sib), device_id_type=MESH)
    for k in range(1, n_grp):
        pl.semaphore_signal(barrier, inc=1, device_id=(lax.rem(g + k, n_grp), b), device_id_type=MESH)
    pl.semaphore_wait(barrier, n_z + n_grp - 1)

    far = []
    for k in range(1, n_z):
        far.append(pltpu.make_async_remote_copy(
            src_ref=coef, dst_ref=table.at[rows(b)], send_sem=gs_sem.at[k], recv_sem=gr_sem.at[k],
            device_id=(g, lax.rem(z + k, n_z) * 2 + c), device_id_type=MESH))
        far[-1].start()
    near = [pltpu.make_async_remote_copy(
        src_ref=coef, dst_ref=table.at[rows(b)], send_sem=fs_sem.at[0], recv_sem=fr_sem.at[0],
        device_id=(g, sib), device_id_type=MESH)]
    near[0].start()

    lane = lax.broadcasted_iota(jnp.int32, (8, NMO), 1)
    kl = lane // IPB
    own = jnp.zeros((8, NMO), jnp.int32)
    for k in range(IJB):
        own = jnp.where(kl == k, owner[k], own)
    rank = jnp.zeros((8, NMO), jnp.int32)
    for k in range(IJB):
        rank = rank + jnp.where((own == owner[k]) & (kl > k), 1, 0)
    want = (own * CAP + rank) * IPB + lane % IPB
    row = lax.broadcasted_iota(jnp.int32, (n_grp * WIDE, NMO), 0)
    low = row % 32
    here = ((row // 32) * 8 + (low % 16) // 2) * IPB + (low // 16) * 2 + low % 2
    perm = jnp.where(here == want[0:1, :], 1.0, 0.0).astype(F32).astype(BF)

    for k in range(1, n_z):
        far[k - 1].wait_recv()
        got = rows(lax.rem(z + n_z - k, n_z) * 2 + c)
        near.append(pltpu.make_async_remote_copy(
            src_ref=table.at[got], dst_ref=table.at[got], send_sem=fs_sem.at[k], recv_sem=fr_sem.at[k],
            device_id=(g, sib), device_id_type=MESH))
        near[-1].start()
    keep.wait()
    for k in range(n_z):
        near[k].wait_recv()
    for k in range(1, n_z):
        far[k - 1].wait_send()
    for k in range(n_z):
        near[k].wait_send()

    if unit == SB:
        panels = table
    else:
        each = SB // unit
        for i in range(table.shape[0]):
            panels[i // each, (i % each) * unit:(i % each + 1) * unit, :] = table[i]
    for t in range(KT):
        la = panels[tile_blocks[t, 0]]
        lat[:, t * SB:(t + 1) * SB] = lax.dot_general(
            perm, la, (((1,), (1,)), ((), ())), preferred_element_type=F32).astype(BF)
        si[t] = panels[tile_blocks[t, 1]]
    load.wait()

    def piece(peer, ch, k):
        return pltpu.make_async_remote_copy(
            src_ref=send.at[peer, pl.ds(ch * RC, RC)], dst_ref=out.at[g, pl.ds(ch * RC, RC)],
            send_sem=s_sem.at[k, ch], recv_sem=r_sem.at[k, ch],
            device_id=(peer, b), device_id_type=MESH)

    def mine():
        return pltpu.make_async_copy(send.at[g], out.at[g], l_sem)

    def chunk(ch, carry):
        for u in range(RC):
            r = ch * RC + u
            for t in range(KT):
                quarter[u, t * SB:(t + 1) * SB, :] = jnp.dot(
                    iv[t, r], si[t], preferred_element_type=F32).astype(BF)
            half = jnp.dot(lat[...], quarter[u], preferred_element_type=F32)
            for o in range(n_grp):
                for s in range(SG):
                    at = o * WIDE + s * 32
                    even, odd = half[at:at + 16], half[at + 16:at + 32]
                    send[o, r, s * 48:s * 48 + 16, :] = even[:, :LANE].astype(BF)
                    send[o, r, s * 48 + 16:s * 48 + 32, :] = odd[:, :LANE].astype(BF)
                    send[o, r, s * 48 + 32:s * 48 + 48, :] = jnp.concatenate(
                        [even[:, LANE:], odd[:, LANE:]], axis=1).astype(BF)
        for k in range(1, n_grp):
            piece(lax.rem(g + k, n_grp), ch, k).start()
        return carry

    lax.fori_loop(0, NCH, chunk, 0)
    mine().start()

    def drain(ch, carry):
        for k in range(1, n_grp):
            copy = piece(lax.rem(g + k, n_grp), ch, k)
            copy.wait_send()
            copy.wait_recv()
        return carry

    lax.fori_loop(0, NCH, drain, 0)
    mine().wait()


def unpack(x_ref, o_ref, rows):
    for r in range(R):
        rows[pl.ds(r, 48, stride=R), :] = x_ref[0, r].astype(F32)
    for s in range(8):
        for q in range(2):
            i = s * 2 + q
            tail = rows[pl.ds((32 + i) * R, R), :]
            o_ref[s, 0, q, :, :LANE] = rows[pl.ds(i * R, R), :].astype(BF)
            o_ref[s, 0, 2 + q, :, :LANE] = rows[pl.ds((16 + i) * R, R), :].astype(BF)
            o_ref[s, 0, q, :, LANE:] = tail[:, :HALF].astype(BF)
            o_ref[s, 0, 2 + q, :, LANE:] = tail[:, HALF:].astype(BF)


def body(n_grp, n_blk, integrals, coefficients, tile_blocks, block_owner):
    anyspace = pl.BlockSpec(memory_space=pl.ANY)
    smem = pl.BlockSpec(memory_space=pltpu.SMEM)
    n_z = n_blk // 2
    depth = coefficients.shape[0]
    unit = math.gcd(depth, SB)
    total = n_blk * depth
    packed = pl.pallas_call(
        functools.partial(exchange, n_grp, n_blk),
        out_shape=jax.ShapeDtypeStruct((n_grp, R, PACK, LANE), BF),
        in_specs=[anyspace, pl.BlockSpec(memory_space=pltpu.VMEM), smem, smem],
        out_specs=anyspace,
        scratch_shapes=[
            pltpu.VMEM((KT, R, SB, SB), BF),
            pltpu.VMEM((total // unit, unit, NMO), BF),
            pltpu.VMEM((1 if unit == SB else total // SB, SB, NMO), BF),
            pltpu.VMEM((KT, SB, NMO), BF),
            pltpu.VMEM((n_grp * WIDE, KT * SB), BF),
            pltpu.VMEM((RC, KT * SB, NMO), BF),
            pltpu.VMEM((n_grp, R, PACK, LANE), BF),
            pltpu.SemaphoreType.DMA,
            pltpu.SemaphoreType.DMA,
            pltpu.SemaphoreType.DMA((n_z,)),
            pltpu.SemaphoreType.DMA((n_z,)),
            pltpu.SemaphoreType.DMA((n_z,)),
            pltpu.SemaphoreType.DMA((n_z,)),
            pltpu.SemaphoreType.DMA((n_grp, NCH)),
            pltpu.SemaphoreType.DMA((n_grp, NCH)),
            pltpu.SemaphoreType.DMA,
        ],
        compiler_params=pltpu.CompilerParams(
            collective_id=0, has_side_effects=True, vmem_limit_bytes=40 * 2**20),
    )(integrals[0, 0], coefficients.reshape(depth // unit, unit, NMO), tile_blocks[0, 0], block_owner)
    return pl.pallas_call(
        unpack,
        grid=(n_grp, SG),
        out_shape=jax.ShapeDtypeStruct((CAP, n_grp, IPB, R, NMO), BF),
        in_specs=[pl.BlockSpec((1, R, 48, LANE), lambda g, s: (g, 0, s, 0))],
        out_specs=pl.BlockSpec((8, 1, IPB, R, NMO), lambda g, s: (s, g, 0, 0, 0)),
        scratch_shapes=[pltpu.VMEM((48 * R, LANE), F32)],
        compiler_params=pltpu.CompilerParams(vmem_limit_bytes=40 * 2**20),
    )(packed)


def solution(mesh):
    in_specs = (
        P("grp", "blk", None, None, None, None),
        P("blk", None),
        P("grp", "blk", None, None),
        P(),
    )
    out_specs = P("grp", None, None, "blk", None)
    step = functools.partial(body, mesh.shape["grp"], mesh.shape["blk"])
    return jax.shard_map(step, mesh=mesh, in_specs=in_specs, out_specs=out_specs, check_vma=False)
```

time: 164 us -> 79.3 us (0.48)
  waiting for transfers between devices: 123 us -> 0 us
  Pallas kernels: 0 us -> 73 us
  between operations: 13.5 us -> 0.02 us
  matrix products: 8.68 us -> 0 us
  local copies, waits for them, and re-layouts: 12.6 us -> 5.69 us
  other arithmetic: 6.33 us -> 0 us
    all_gather x2 -> x0, waiting for transfers between devices: 122 us -> none  [the longest x1 95.6 us: body(): everyone = lax.all_gather(pair_blocks[:, None], 'grp', axis=1, tiled=True)]
    pallas_call x0 -> x2, Pallas kernels: none -> 73 us  [the longest x1 66.6 us: body(): pl.pallas_call(functools.partial(exchange, n_grp, n_blk), out_shape=jax.S...]
    dot_general x1 -> x0, matrix products: 8.68 us -> none  [body(): jnp.einsum('tai,tarj->irj', la_coef, quarter, preferred_element_type=jnp....]
    gather x3 -> x0, local copies, waits for them, and re-layouts: 8.15 us -> none  [the longest x1 6.87 us: body(): picked = jnp.take(everyone, wanted, axis=0)]
    select_n x1 -> x0, other arithmetic: 5.1 us -> none  [body(): jnp.where(present[:, None, None, None, None], picked, jnp.zeros_like(pick...]
    unnamed x2 -> x5, local copies, waits for them, and re-layouts: 0.01 us -> 4.93 us
    another operation x1 -> x0, local copies, waits for them, and re-layouts: 2.73 us -> none  [body(): everyone = lax.all_gather(pair_blocks[:, None], 'grp', axis=1, tiled=True)]
  transfers between devices with their start and end apart: 2 -> 0, of which waited for: 2 -> 0; matrix products, arithmetic and copies ran while one was open for 1% -> 0% of each run, Pallas kernels for 0% -> 0%
where the time goes in v1:
time: 79.3 us; the launch traced here: 78.7 us
  Pallas kernels  73 us (92%)
  local copies, waits for them, and re-layouts  5.69 us (7%)
    pallas_call x1, Pallas kernels, body(): pl.pallas_call(functools.partial(exchange, n_grp, n_blk), out_shape=jax.S...  66.6 us
    pallas_call x1, Pallas kernels, body(): pl.pallas_call(unpack, grid=(n_grp, SG), out_shape=jax.ShapeDtypeStruct((...  6.34 us
    unnamed x5, local copies, waits for them, and re-layouts  4.93 us

profile of v1, /device:TPU:0, one launch (start us, length us, event | category | flops | bytes accessed | tf_op | source)
XLA Modules:
  0.0 78.7 jit_solution(6130966743364802732)
XLA Ops:
  0.0 0.8 copy.6.tile_blocks
  0.8 1.0 %copy.5 = bf16[384,192]{1,0:T(8,128)(2,1)S(1)} copy(bf16[384,192]{0,1:T(8,128)(2,1)} %param.5) | data formatting | bytes 294912 | tf_op args[1]
  1.8 0.0 copy-start
  1.8 3.2 %copy-done = bf16[1,1,10,24,128,128]{5,4,3,2,1,0:T(8,128)(2,1)S(1)} copy-done((bf16[1,1,10,24,128,128]{5,4,3,2,1,0:T(8,128)(2,1)S(1)}, bf16[1,1,10,24,128,128]{5,4,3,2,1,0:T(8,128)(2,1)}, u32[]{:S(2)}) %copy-start) | copy-done | bytes 7864344
  5.1 0.0 copy-start.1
  5.1 0.7 copy-done.1
  5.7 66.6 %shard_map.46.x_ref = bf16[4,24,144,128]{3,2,1,0:T(8,128)(2,1)S(1)} custom-call(bf16[10,24,128,128]{3,2,1,0:T(8,128)(2,1)S(1)} %bitcast.3, bf16[3,128,192]{2,1,0:T(8,128)(2,1)S(1)} %bitcast.4, s32[10,2]{1,0:T(8,128)S(1)} %copy.6.tile_blocks, s32[48]{0:T(128)S(1)} %copy-done.1), custom_call_target="tpu_custom_call" | custom-call | tf_op jit(solution)/shard_map/pallas_call | solution.py:175
  72.4 6.3 %shard_map.47 = bf16[24,4,4,24,192]{4,3,2,1,0:T(8,128)(2,1)} custom-call(bf16[4,24,144,128]{3,2,1,0:T(8,128)(2,1)S(1)} %shard_map.46.x_ref), custom_call_target="tpu_custom_call" | custom-call | tf_op jit(solution)/shard_map/pallas_call | solution.py:201
Async XLA Ops:
  1.8 3.2 %copy-start = (bf16[1,1,10,24,128,128]{5,4,3,2,1,0:T(8,128)(2,1)S(1)}, bf16[1,1,10,24,128,128]{5,4,3,2,1,0:T(8,128)(2,1)}, u32[]{:S(2)}) copy-start(bf16[1,1,10,24,128,128]{5,4,3,2,1,0:T(8,128)(2,1)} %param.4) | copy-start | bytes 23592964
  5.1 0.7 copy-start.1

commit v2 on v1

--- a/solution.py
+++ b/solution.py
@@ -30,7 +30,7 @@
 def exchange(
     n_grp, n_blk, ints, coef, tile_blocks, owner, out,
     iv, table, panels, si, lat, quarter, send,
-    int_sem, own_sem, gs_sem, gr_sem, fs_sem, fr_sem, s_sem, r_sem, l_sem,
+    int_sem, own_sem, gs_sem, gr_sem, xs_sem, xr_sem, fs_sem, fr_sem, s_sem, r_sem, l_sem,
 ):
     g = lax.axis_index("grp")
     b = lax.axis_index("blk")
@@ -43,6 +43,13 @@
     load = pltpu.make_async_copy(ints, iv, int_sem)
     load.start()
 
+    split = unit % (16 * n_grp) == 0
+    sub = unit // n_grp if split else unit
+
+    def shard(ref, first, grp):
+        part = pl.ds(pl.multiple_of(grp * sub, 16), sub) if split else pl.ds(0, unit)
+        return ref.at[pl.ds(first, depth), part]
+
     def rows(blk):
         return pl.ds(blk * depth, depth)
 
@@ -60,11 +67,12 @@
     far = []
     for k in range(1, n_z):
         far.append(pltpu.make_async_remote_copy(
-            src_ref=coef, dst_ref=table.at[rows(b)], send_sem=gs_sem.at[k], recv_sem=gr_sem.at[k],
+            src_ref=shard(coef, 0, g), dst_ref=shard(table, b * depth, g),
+            send_sem=gs_sem.at[k], recv_sem=gr_sem.at[k],
             device_id=(g, lax.rem(z + k, n_z) * 2 + c), device_id_type=MESH))
         far[-1].start()
     near = [pltpu.make_async_remote_copy(
-        src_ref=coef, dst_ref=table.at[rows(b)], send_sem=fs_sem.at[0], recv_sem=fr_sem.at[0],
+        src_ref=coef, dst_ref=table.at[rows(b)], send_sem=fs_sem.at[0, 0], recv_sem=fr_sem.at[0, 0],
         device_id=(g, sib), device_id_type=MESH)]
     near[0].start()
 
@@ -82,20 +90,34 @@
     here = ((row // 32) * 8 + (low % 16) // 2) * IPB + (low // 16) * 2 + low % 2
     perm = jnp.where(here == want[0:1, :], 1.0, 0.0).astype(F32).astype(BF)
 
+    def forward(k, j):
+        ref = shard(table, (lax.rem(z + n_z - k, n_z) * 2 + c) * depth, lax.rem(g + n_grp - j, n_grp))
+        near.append(pltpu.make_async_remote_copy(
+            src_ref=ref, dst_ref=ref, send_sem=fs_sem.at[k, j], recv_sem=fr_sem.at[k, j],
+            device_id=(g, sib), device_id_type=MESH))
+        near[-1].start()
+
+    across = []
     for k in range(1, n_z):
         far[k - 1].wait_recv()
-        got = rows(lax.rem(z + n_z - k, n_z) * 2 + c)
-        near.append(pltpu.make_async_remote_copy(
-            src_ref=table.at[got], dst_ref=table.at[got], send_sem=fs_sem.at[k], recv_sem=fr_sem.at[k],
-            device_id=(g, sib), device_id_type=MESH))
-        near[-1].start()
+        if split:
+            ref = shard(table, (lax.rem(z + n_z - k, n_z) * 2 + c) * depth, g)
+            for j in range(1, n_grp):
+                across.append(pltpu.make_async_remote_copy(
+                    src_ref=ref, dst_ref=ref, send_sem=xs_sem.at[k, j], recv_sem=xr_sem.at[k, j],
+                    device_id=(lax.rem(g + j, n_grp), b), device_id_type=MESH))
+                across[-1].start()
+        forward(k, 0)
+    if split:
+        for k in range(1, n_z):
+            for j in range(1, n_grp):
+                across[(k - 1) * (n_grp - 1) + j - 1].wait_recv()
+                forward(k, j)
     keep.wait()
-    for k in range(n_z):
-        near[k].wait_recv()
-    for k in range(1, n_z):
-        far[k - 1].wait_send()
-    for k in range(n_z):
-        near[k].wait_send()
+    for copy in near:
+        copy.wait_recv()
+    for copy in far + across + near:
+        copy.wait_send()
 
     if unit == SB:
         panels = table
@@ -166,7 +188,7 @@
 
 
 def body(n_grp, n_blk, integrals, coefficients, tile_blocks, block_owner):
-    anyspace = pl.BlockSpec(memory_space=pl.ANY)
+    hbm = pl.BlockSpec(memory_space=pltpu.HBM)
     smem = pl.BlockSpec(memory_space=pltpu.SMEM)
     n_z = n_blk // 2
     depth = coefficients.shape[0]
@@ -175,8 +197,8 @@
     packed = pl.pallas_call(
         functools.partial(exchange, n_grp, n_blk),
         out_shape=jax.ShapeDtypeStruct((n_grp, R, PACK, LANE), BF),
-        in_specs=[anyspace, pl.BlockSpec(memory_space=pltpu.VMEM), smem, smem],
-        out_specs=anyspace,
+        in_specs=[hbm, hbm, smem, smem],
+        out_specs=hbm,
         scratch_shapes=[
             pltpu.VMEM((KT, R, SB, SB), BF),
             pltpu.VMEM((total // unit, unit, NMO), BF),
@@ -189,8 +211,10 @@
             pltpu.SemaphoreType.DMA,
             pltpu.SemaphoreType.DMA((n_z,)),
             pltpu.SemaphoreType.DMA((n_z,)),
-            pltpu.SemaphoreType.DMA((n_z,)),
-            pltpu.SemaphoreType.DMA((n_z,)),
+            pltpu.SemaphoreType.DMA((n_z, n_grp)),
+            pltpu.SemaphoreType.DMA((n_z, n_grp)),
+            pltpu.SemaphoreType.DMA((n_z, n_grp)),
+            pltpu.SemaphoreType.DMA((n_z, n_grp)),
             pltpu.SemaphoreType.DMA((n_grp, NCH)),
             pltpu.SemaphoreType.DMA((n_grp, NCH)),
             pltpu.SemaphoreType.DMA,

time: 79.3 us -> 75.3 us (0.950)
  Pallas kernels: 73 us -> 69.4 us
    pallas_call x1, Pallas kernels: 66.6 us -> 63 us  [body(): pl.pallas_call(functools.partial(exchange, n_grp, n_blk), out_shape=jax.S...]
where the time goes in v2:
time: 75.3 us; the launch traced here: 75.1 us
  Pallas kernels  69.4 us (92%)
  local copies, waits for them, and re-layouts  5.69 us (8%)
    pallas_call x1, Pallas kernels, body(): pl.pallas_call(functools.partial(exchange, n_grp, n_blk), out_shape=jax.S...  63 us
    pallas_call x1, Pallas kernels, body(): pl.pallas_call(unpack, grid=(n_grp, SG), out_shape=jax.ShapeDtypeStruct((...  6.34 us
    unnamed x5, local copies, waits for them, and re-layouts  4.93 us

profile of v2, /device:TPU:0, one launch (start us, length us, event | category | flops | bytes accessed | tf_op | source)
XLA Modules:
  0.0 75.1 jit_solution(6242024577444648936)
XLA Ops:
  0.0 0.8 %copy.6.tile_blocks = s32[10,2]{1,0:T(8,128)S(1)} copy(s32[10,2]{0,1:T(2,128)} %bitcast.5) | data formatting | bytes 160 | tf_op jit(solution)/shard_map/squeeze | solution.py:224
  0.8 1.0 %copy.5 = bf16[384,192]{1,0:T(8,128)(2,1)S(1)} copy(bf16[384,192]{0,1:T(8,128)(2,1)} %param.5) | data formatting | bytes 294912 | tf_op args[1]
  1.8 0.0 copy-start
  1.8 3.2 %copy-done = bf16[1,1,10,24,128,128]{5,4,3,2,1,0:T(8,128)(2,1)S(1)} copy-done((bf16[1,1,10,24,128,128]{5,4,3,2,1,0:T(8,128)(2,1)S(1)}, bf16[1,1,10,24,128,128]{5,4,3,2,1,0:T(8,128)(2,1)}, u32[]{:S(2)}) %copy-start) | copy-done | bytes 7864344
  5.1 0.0 copy-start.1
  5.1 0.7 copy-done.1
  5.7 63.0 %shard_map.46.x_ref = bf16[4,24,144,128]{3,2,1,0:T(8,128)(2,1)S(1)} custom-call(bf16[10,24,128,128]{3,2,1,0:T(8,128)(2,1)S(1)} %bitcast.3, bf16[3,128,192]{2,1,0:T(8,128)(2,1)S(1)} %bitcast.4, s32[10,2]{1,0:T(8,128)S(1)} %copy.6.tile_blocks, s32[48]{0:T(128)S(1)} %copy-done.1), custom_call_target="tpu_custom_call" | custom-call | tf_op jit(solution)/shard_map/pallas_call | solution.py:197
  68.8 6.3 %shard_map.47 = bf16[24,4,4,24,192]{4,3,2,1,0:T(8,128)(2,1)} custom-call(bf16[4,24,144,128]{3,2,1,0:T(8,128)(2,1)S(1)} %shard_map.46.x_ref), custom_call_target="tpu_custom_call" | custom-call | tf_op jit(solution)/shard_map/pallas_call | solution.py:225
Async XLA Ops:
  1.8 3.2 %copy-start = (bf16[1,1,10,24,128,128]{5,4,3,2,1,0:T(8,128)(2,1)S(1)}, bf16[1,1,10,24,128,128]{5,4,3,2,1,0:T(8,128)(2,1)}, u32[]{:S(2)}) copy-start(bf16[1,1,10,24,128,128]{5,4,3,2,1,0:T(8,128)(2,1)} %param.4) | copy-start | bytes 23592964
  5.1 0.7 copy-start.1
